TPU v7x, 32 devices: a whole 2x2x4 slice. The times are simulated.
32 devices in a mesh: tm: 4 (over x, core), band: 8 (over z, y).
Axes of the slice: x: 2, y: 2, z: 4, core: 2. Of those that a mesh axis runs over, the one named last changes fastest.
Arguments:
- volts: bfloat16 [2, 1024, 262144], P(None, 'band', 'tm'), may hold values from -4 to 4
- taps: float32 [8, 256], replicated, may hold values from -2 to 2
Outputs:
- visibilities: float32 [256, 2, 1024, 1024], P(('tm', 'band'))
All inputs are finite; a program needn't handle non-finite values.
Results may differ from a plain program's by a relative error of at most 0.0046.
Values may be sent and summed in bfloat16 or wider, within the bound.
A program may use at most 256 MiB of HBM per device.

v0:
```python
import math

import jax
import jax.numpy as jnp
from jax import lax
from jax.sharding import PartitionSpec as P


def shifted(shard, axis, by):
    size = lax.axis_size(axis)
    pairs = [(i, i + by) for i in range(size) if 0 <= i + by < size]
    return lax.ppermute(shard, axis, pairs)


def dft_table(channels):
    index = jnp.arange(channels, dtype=jnp.int32)
    turns = index[:, None] * index[None, :] % channels
    theta = turns.astype(jnp.float32) * (2.0 * math.pi / channels)
    factor = 1.0 / math.sqrt(channels)
    cosine = jnp.cos(theta) * factor
    sine = jnp.sin(theta) * factor
    real_row = jnp.stack([cosine, sine], axis=1)
    imag_row = jnp.stack([-sine, cosine], axis=1)
    table = jnp.stack([real_row, imag_row], axis=1)
    return table.reshape(2 * channels, 2, channels).astype(jnp.bfloat16)


def weighting(signal):
    swapped = jnp.stack([signal[:, 1], -signal[:, 0]], axis=1)
    return jnp.stack([signal, swapped], axis=1)


def square_products(signal):
    return jnp.einsum(
        "corps,crqs->copq", weighting(signal), signal, preferred_element_type=jnp.float32
    )


def correlate(signal):
    return square_products(signal)


def per_device(volts, taps):
    time_groups = lax.axis_size("tm")
    band_groups = lax.axis_size("band")
    taps_count = taps.shape[0]
    channels = taps.shape[1]
    local_inputs = volts.shape[1]
    samples = volts.shape[2]
    spec_local = samples // channels
    own_channels = channels // (time_groups * band_groups)
    margin = (taps_count - 1) * channels
    history = shifted(volts[:, :, samples - margin :], "tm", 1)
    frames = jnp.concatenate([history, volts], axis=2)
    frames = frames.reshape(2, local_inputs, spec_local + taps_count - 1, channels).astype(
        jnp.float32
    )
    filtered = taps[0] * frames[:, :, 0:spec_local, :]
    for weight_index in range(1, taps_count):
        filtered = (
            filtered
            + taps[weight_index] * frames[:, :, weight_index : weight_index + spec_local, :]
        )
    filtered = filtered.astype(jnp.bfloat16)
    table = dft_table(channels)
    spectra = lax.dot_general(
        table, filtered, (((1, 2), (0, 3)), ((), ())), preferred_element_type=jnp.float32
    )
    spectra = spectra.astype(jnp.bfloat16).reshape(
        time_groups, band_groups, own_channels, 2, local_inputs, spec_local
    )
    spectra_total = spec_local * time_groups
    turned = lax.all_to_all(
        lax.all_to_all(spectra, "tm", split_axis=0, concat_axis=5, tiled=True),
        "band",
        split_axis=1,
        concat_axis=4,
        tiled=True,
    )
    result = correlate(turned.reshape(own_channels, 2, turned.shape[4], spectra_total))
    return result * (1.0 / spectra_total)


def solution(mesh):
    in_specs = (P(None, "band", "tm"), P())
    out_specs = P(("tm", "band"), None, None, None)
    return jax.shard_map(
        per_device, mesh=mesh, in_specs=in_specs, out_specs=out_specs, check_vma=False
    )
```

profile of v0, /device:TPU:3, one launch (start us, length us, event | category | flops | bytes accessed | tf_op | source)
XLA Modules:
  0.0 1703.4 jit_solution(10425935168011187321)
XLA Ops:
  0.0 0.0 copy-start.1
  0.0 41.1 %copy.22 = bf16[2,128,65536]{1,2,0:T(8,128)(2,1)} copy(bf16[2,128,65536]{2,1,0:T(8,128)(2,1)} %param.2) | data formatting | bytes 67108864 | tf_op args[0]
  41.1 1.2 slice.76
  42.3 1.3 collective-permute-start
  43.6 1.0 fusion.18
  44.6 1.1 negate_convert_fusion
  45.8 0.1 pad_maximum_fusion.2
  45.8 0.5 copy.21
  46.4 1.0 reshape.105
  47.4 0.0 copy-done.1
  47.4 0.0 collective-permute-done
  47.4 23.3 %pad_maximum_fusion.1 = bf16[2,128,67328]{1,2,0:T(8,128)(2,1)} fusion(bf16[2,128,65536]{1,2,0:T(8,128)(2,1)} %copy.22, bf16[2,128,1792]{1,2,0:T(8,128)(2,1)S(1)} %collective-permute-done), kind=kLoop, calls=%fused_computation.21 | loop fusion | flops 68943872 | bytes 68943872 | tf_op jit(solution)/shard_map/concatenate | solution.py:54
  70.7 33.9 %convert.20 = f32[2,128,263,256]{1,3,2,0:T(8,128)} convert(bf16[2,128,263,256]{1,3,2,0:T(8,128)(2,1)} %bitcast.46) | non-fusion elementwise | flops 17235968 | bytes 103415808 | tf_op jit(solution)/shard_map/convert_element_type | solution.py:55
  104.6 173.0 %fusion.1 = bf16[2,128,256,256]{1,3,2,0:T(8,128)(2,1)} fusion(f32[2,128,263,256]{1,3,2,0:T(8,128)} %convert.20, f32[256]{0:T(256)S(1)} %bitcast.59, f32[256]{0:T(256)S(1)} %bitcast.60, f32[256]{0:T(256)S(1)} %bitcast.54, f32[256]{0:T(256)S(1)} %bitcast.55, f32[256]{0:T(256)S(1)} %bitcast.56, f32[256]{0:T(256)S(1)} %bitcast.57, f32[256]{0:T(256)S(1)} %bitcast.58, ...), kind=kLoop, calls=%fused_computation.2 | loop fusion | flops 268435456 | bytes 570433536 | tf_op jit(solution)/shard_map/convert_element_type | solution.py:64
  277.6 0.0 copy-start
  277.6 43.8 %copy.24 = bf16[2,128,256,256]{3,2,0,1:T(8,128)(2,1)} copy(bf16[2,128,256,256]{1,3,2,0:T(8,128)(2,1)} %fusion.1) | data formatting | bytes 67108864 | tf_op jit(solution)/shard_map/convert_element_type | solution.py:64
  321.4 0.0 copy-done
  321.4 30.4 %bitcast_convert_fusion = bf16[512,128,256]{2,0,1:T(8,128)(2,1)} fusion(bf16[512,2,256,1]{2,0,1,3:T(8,128)(2,1)S(1)} %copy-done, bf16[2,128,256,256]{3,2,0,1:T(8,128)(2,1)} %copy.24), kind=kOutput, calls=%fused_computation.18 | convolution fusion | flops 17196646400 | bytes 67633152 | tf_op jit(solution)/shard_map/dot_general | solution.py:66
  351.8 44.2 %copy.34 = bf16[512,128,256]{1,2,0:T(8,128)(2,1)} copy(bf16[512,128,256]{2,0,1:T(8,128)(2,1)} %bitcast_convert_fusion) | data formatting | bytes 67108864 | tf_op jit(solution)/shard_map/reshape | solution.py:69
  396.0 379.7 %all_to_all.33 = bf16[4,8,8,2,128,256]{4,5,3,2,1,0:T(8,128)(2,1)} all-to-all(bf16[4,8,8,2,128,256]{4,5,3,2,1,0:T(8,128)(2,1)} %bitcast.50), channel_id=1, replica_groups=mesh['tm'=4,'band'=8] {'tm'}, dimensions={0} | all-to-all | bytes 67108864 | tf_op jit(solution)/shard_map/all_to_all | solution.py:74
  775.7 22.8 %copy.26 = bf16[4,8,8,2,128,256]{4,5,0,3,2,1:T(8,128)(2,1)} copy(bf16[4,8,8,2,128,256]{4,5,3,2,1,0:T(8,128)(2,1)} %all_to_all.33) | data formatting | bytes 67108864 | tf_op jit(solution)/shard_map/all_to_all | solution.py:74
  798.5 734.3 %all_to_all.34 = bf16[1,8,8,2,128,1024]{4,5,3,2,0,1:T(8,128)(2,1)} all-to-all(bf16[1,8,8,2,128,1024]{4,5,3,2,0,1:T(8,128)(2,1)} %bitcast.51), channel_id=1, replica_groups=mesh['tm'=4,'band'=8] {'band'}, dimensions={1} | all-to-all | bytes 67108864 | tf_op jit(solution)/shard_map/all_to_all | solution.py:73
  1532.8 42.1 %copy.28 = bf16[1,1,8,2,8,128,1024]{6,5,4,3,2,1,0:T(8,128)(2,1)} copy(bf16[1,1,8,2,8,128,1024]{5,6,3,2,4,1,0:T(8,128)(2,1)} %bitcast.52) | data formatting | bytes 67108864 | tf_op jit(solution)/shard_map/all_to_all | solution.py:73
  1574.9 22.5 %fusion.19 = (bf16[8,1,1024,1024]{3,2,1,0:T(8,128)(2,1)}, bf16[8,1,1024,1024]{3,2,1,0:T(8,128)(2,1)}) fusion(bf16[8,2,1024,1024]{3,2,1,0:T(8,128)(2,1)} %bitcast.47), kind=kLoop, calls=%fused_computation.40 | loop fusion | flops 8388608 | bytes 67108864 | tf_op jit(solution)/shard_map/slice | solution.py:29
  1597.4 23.0 %maximum_bitcast_fusion = bf16[8,1,2,1024,1024]{4,3,2,0,1:T(8,128)(2,1)} fusion(bf16[8,1,1024,1024]{3,2,1,0:T(8,128)(2,1)} %get-tuple-element.6, bf16[8,1,1024,1024]{3,2,1,0:T(8,128)(2,1)} %get-tuple-element.5), kind=kLoop, calls=%fused_computation.22 | loop fusion | flops 16777216 | bytes 67108864 | tf_op jit(solution)/shard_map/stack | solution.py:30
  1620.4 83.0 %bitcast_multiply_fusion = f32[8,2,1024,1024]{3,2,1,0:T(8,128)} fusion(bf16[8,2,1024,1024,1]{3,2,1,4,0:T(8,128)(2,1)} %bitcast.48, bf16[8,1,2,1024,1024]{4,3,2,0,1:T(8,128)(2,1)} %maximum_bitcast_fusion, bf16[8,1,2,1024,1024]{4,3,2,0,1:T(8,128)(2,1)} %bitcast.49), kind=kOutput, calls=%fused_computation.17 | convolution fusion | flops 68769808384 | bytes 167772160 | tf_op jit(solution)/shard_map/corps,crqs->copq/dot_general | solution.py:34
  (2 shorter events, 0.0 us)
Async XLA Ops:
  0.0 47.4 %copy-start.1 = (f32[8,256]{1,0:T(8,128)S(1)}, f32[8,256]{1,0:T(8,128)}, u32[]{:S(2)}) copy-start(f32[8,256]{1,0:T(8,128)} %param.3) | copy-start | bytes 24580
  42.3 5.1 collective-permute-start
  277.6 43.8 %copy-start = (bf16[512,2,256,1]{2,0,1,3:T(8,128)(2,1)S(1)}, bf16[512,2,256,1]{2,0,1,3:T(8,128)(2,1)}, u32[]{:S(2)}) copy-start(bf16[512,2,256,1]{2,0,1,3:T(8,128)(2,1)} %reshape.105) | copy-start | bytes 1572868
where the time goes:
time: 1710 us; the launch traced here: 1700 us
  blocking collectives  1110 us (65%)
  other arithmetic  278 us (16%)
  local copies, waits for them, and re-layouts  197 us (12%)
  matrix products  113 us (7%)
    all_to_all x1, blocking collectives, per_device(): lax.all_to_all(lax.all_to_all(spectra, 'tm', split_axis=0, concat_axis=5,...  734 us
    all_to_all x1, blocking collectives, per_device(): lax.all_to_all(spectra, 'tm', split_axis=0, concat_axis=5, tiled=True)  380 us
    convert_element_type x1, other arithmetic, per_device(): filtered = filtered.astype(jnp.bfloat16)  173 us
    dot_general x1, matrix products, square_products(): jnp.einsum('corps,crqs->copq', weighting(signal), signal, preferred_eleme...  83 us
    reshape x1, local copies, waits for them, and re-layouts, per_device(): spectra.astype(jnp.bfloat16)  44.2 us
    convert_element_type x1, local copies, waits for them, and re-layouts, per_device(): filtered = filtered.astype(jnp.bfloat16)  43.8 us
    all_to_all x1, local copies, waits for them, and re-layouts, per_device(): lax.all_to_all(lax.all_to_all(spectra, 'tm', split_axis=0, concat_axis=5,...  42.1 us
    unnamed x5, local copies, waits for them, and re-layouts  41.1 us
  transfers between devices with their start and end apart: 1, of which 0 were waited for; matrix products, arithmetic and copies ran while one was open for 0% of the time, Pallas kernels for 0%

commit v1 on v0

--- a/solution.py
+++ b/solution.py
@@ -1,8 +1,11 @@
+import functools
 import math
 
 import jax
 import jax.numpy as jnp
 from jax import lax
+from jax.experimental import pallas as pl
+from jax.experimental.pallas import tpu as pltpu
 from jax.sharding import PartitionSpec as P
 
 
@@ -40,7 +43,327 @@
     return square_products(signal)
 
 
+STEP = 16
+STRIP = 16
+LANES = 128
+BLOCK = 256
+MESH = pl.DeviceIdType.MESH
+
+
+def filter_block(volts_ref, history_ref, taps_ref, filtered_ref, steps):
+    taps_count, channels = taps_ref.shape
+    inputs = history_ref.shape[1]
+    margin = taps_count - 1
+
+    def strip(index, carry):
+        rows = pl.ds(pl.multiple_of(index * STRIP, STRIP), STRIP)
+        for part in range(2):
+            for lane in range(0, channels, LANES):
+                weights = [
+                    jnp.broadcast_to(taps_ref[j : j + 1, lane : lane + LANES], (STRIP, LANES))
+                    for j in range(taps_count)
+                ]
+                frames = []
+                for f in range(steps + margin):
+                    ref, at = (history_ref, f) if f < margin else (volts_ref, f - margin)
+                    start = at * channels + lane
+                    frames.append(ref[part, rows, start : start + LANES].astype(jnp.float32))
+                for t in range(steps):
+                    total = weights[0] * frames[t]
+                    for j in range(1, taps_count):
+                        total = total + weights[j] * frames[t + j]
+                    out_rows = pl.ds(pl.multiple_of(t * inputs + index * STRIP, STRIP), STRIP)
+                    column = part * channels + lane
+                    filtered_ref[out_rows, column : column + LANES] = total.astype(jnp.bfloat16)
+        return carry
+
+    lax.fori_loop(0, inputs // STRIP, strip, 0)
+
+
+def transform_block(table_ref, filtered_ref, turned_ref, steps, inputs):
+    rows = table_ref.shape[0]
+    for t in range(0, steps, 2):
+        product = lax.dot_general(
+            table_ref[...],
+            filtered_ref[t * inputs : (t + 2) * inputs, :],
+            (((1,), (1,)), ((), ())),
+            preferred_element_type=jnp.float32,
+        )
+        turned_ref[pl.ds(t, rows, stride=steps), :] = product[:, :inputs]
+        turned_ref[pl.ds(t + 1, rows, stride=steps), :] = product[:, inputs:]
+
+
+def exchange_kernel(
+    groups,
+    volts_ref,
+    history_in_ref,
+    taps_ref,
+    table_ref,
+    arrived_ref,
+    volts_buf,
+    history,
+    filtered,
+    turned,
+    spectra,
+    in_sem,
+    send_sem,
+    recv_sem,
+    local_sem,
+):
+    time_groups, band_groups = groups
+    devices = time_groups * band_groups
+    my_time = lax.axis_index("tm")
+    my_band = lax.axis_index("band")
+    me = my_time * band_groups + my_band
+    blocks, _, planes, steps, inputs = spectra.shape
+    channels = taps_ref.shape[1]
+    width = steps * channels
+
+    def offset(k):
+        turn = lax.rem(k, band_groups)
+        half = turn // 2
+        parity = lax.rem(turn, 2)
+        by_band = lax.rem(band_groups // 2 + half + parity * (band_groups // 2), band_groups)
+        by_time = lax.rem(k // band_groups + turn, time_groups)
+        return by_time, by_band
+
+    def fetch(block):
+        slot = lax.rem(block, 2)
+        columns = pl.ds(pl.multiple_of(block * width, LANES), width)
+        return pltpu.make_async_copy(
+            volts_ref.at[:, :, columns], volts_buf.at[slot], in_sem.at[slot]
+        )
+
+    fetch(0).start()
+    history[...] = history_in_ref[...]
+
+    barrier = pltpu.get_barrier_semaphore()
+
+    def greet(k, carry):
+        there_time = lax.rem(my_time + k // band_groups, time_groups)
+        there_band = lax.rem(my_band + lax.rem(k, band_groups), band_groups)
+        pl.semaphore_signal(
+            barrier, inc=1, device_id=(there_time, there_band), device_id_type=MESH
+        )
+        return carry
+
+    lax.fori_loop(1, devices, greet, 0)
+    pl.semaphore_wait(barrier, devices - 1)
+
+    def step(block, carry):
+        slot = lax.rem(block, 2)
+        fetch(block).wait()
+
+        @pl.when(block + 1 < blocks)
+        def _():
+            fetch(block + 1).start()
+
+        filter_block(volts_buf.at[slot], history, taps_ref, filtered, steps)
+        margin = history.shape[2]
+        history[...] = volts_buf[slot, :, :, width - margin :]
+        transform_block(table_ref, filtered, turned, steps, inputs)
+
+        def pack(there, carry):
+            rows = pl.ds(pl.multiple_of(there * (planes * steps), STRIP), planes * steps)
+            values = turned[rows, :].reshape(planes, steps, inputs)
+            spectra[block, there] = values.astype(jnp.bfloat16)
+            return carry
+
+        lax.fori_loop(0, devices, pack, 0)
+
+        def send(k, carry):
+            by_time, by_band = offset(k)
+            there_time = lax.rem(my_time + by_time, time_groups)
+            there_band = lax.rem(my_band + by_band, band_groups)
+            there = there_time * band_groups + there_band
+
+            @pl.when(there != me)
+            def _():
+                pltpu.make_async_remote_copy(
+                    src_ref=spectra.at[block, there],
+                    dst_ref=arrived_ref.at[me, block],
+                    send_sem=send_sem.at[there],
+                    recv_sem=recv_sem.at[me],
+                    device_id=(there_time, there_band),
+                    device_id_type=MESH,
+                ).start()
+
+            return carry
+
+        lax.fori_loop(0, devices, send, 0)
+        return carry
+
+    lax.fori_loop(0, blocks, step, 0)
+    own = pltpu.make_async_copy(spectra.at[:, me], arrived_ref.at[me], local_sem)
+    own.start()
+
+    def finish(k, carry):
+        there_time = lax.rem(my_time + k // band_groups, time_groups)
+        there_band = lax.rem(my_band + lax.rem(k, band_groups), band_groups)
+        there = there_time * band_groups + there_band
+        pltpu.make_async_copy(spectra.at[:, there], arrived_ref.at[there], send_sem.at[there]).wait()
+        pltpu.make_async_copy(spectra.at[:, there], arrived_ref.at[there], recv_sem.at[there]).wait()
+        return carry
+
+    lax.fori_loop(1, devices, finish, 0)
+    own.wait()
+
+
+def exchanged(volts, history, taps, groups):
+    devices = groups[0] * groups[1]
+    taps_count, channels = taps.shape
+    inputs = volts.shape[1]
+    blocks = volts.shape[2] // (channels * STEP)
+    planes = 2 * channels // devices
+    table = dft_table(channels).reshape(2 * channels, 2 * channels)
+    dtype = jnp.bfloat16
+    return pl.pallas_call(
+        functools.partial(exchange_kernel, groups),
+        out_shape=jax.ShapeDtypeStruct((devices, blocks, planes, STEP, inputs), dtype),
+        in_specs=[pl.BlockSpec(memory_space=pl.ANY)]
+        + [pl.BlockSpec(memory_space=pltpu.VMEM)] * 3,
+        out_specs=pl.BlockSpec(memory_space=pl.ANY),
+        scratch_shapes=[
+            pltpu.VMEM((2, 2, inputs, STEP * channels), dtype),
+            pltpu.VMEM(history.shape, dtype),
+            pltpu.VMEM((STEP * inputs, 2 * channels), dtype),
+            pltpu.VMEM((2 * channels * STEP, inputs), jnp.float32),
+            pltpu.VMEM((blocks, devices, planes, STEP, inputs), dtype),
+            pltpu.SemaphoreType.DMA((2,)),
+            pltpu.SemaphoreType.DMA((devices,)),
+            pltpu.SemaphoreType.DMA((devices,)),
+            pltpu.SemaphoreType.DMA,
+        ],
+        compiler_params=pltpu.CompilerParams(
+            collective_id=0, has_side_effects=True, vmem_limit_bytes=58 * 1024 * 1024
+        ),
+        cost_estimate=pl.CostEstimate(
+            flops=8 * channels * volts.size,
+            bytes_accessed=4 * volts.size,
+            transcendentals=0,
+        ),
+    )(volts, history, taps, table)
+
+
+def correlate_kernel(groups, scale, arrived_ref, result_ref, signal, across, sems):
+    time_groups, band_groups = groups
+    channel = pl.program_id(0)
+    count = pl.num_programs(0)
+    _, blocks, _, steps, inputs = arrived_ref.shape
+    total_inputs = signal.shape[4]
+    length = time_groups * blocks * steps
+
+    def load(which, slot):
+        def one(there, carry):
+            at_time = there // band_groups
+            at_band = lax.rem(there, band_groups)
+            lanes = pl.ds(pl.multiple_of(at_band * inputs, LANES), inputs)
+            pltpu.make_async_copy(
+                arrived_ref.at[there, :, pl.ds(which * 2, 2)],
+                signal.at[slot, pl.ds(at_time * blocks, blocks), :, :, lanes],
+                sems.at[slot],
+            ).start()
+            return carry
+
+        lax.fori_loop(0, time_groups * band_groups, one, 0)
+
+    slot = lax.rem(channel, 2)
+
+    @pl.when(channel == 0)
+    def _():
+        load(0, 0)
+
+    @pl.when(channel + 1 < count)
+    def _():
+        load(channel + 1, lax.rem(channel + 1, 2))
+
+    pltpu.make_async_copy(signal.at[slot], signal.at[slot], sems.at[slot]).wait()
+
+    def turn(index, carry):
+        at = pl.multiple_of(index * LANES, LANES)
+        for part in range(2):
+            piece = signal[slot, :, part, :, pl.ds(at, LANES)].reshape(length, LANES)
+            across[part, pl.ds(at, LANES), :] = piece.T
+        return carry
+
+    lax.fori_loop(0, total_inputs // LANES, turn, 0)
+
+    def product(left, right, p, q):
+        return jnp.dot(
+            across[left, p, :],
+            signal[slot, :, right, :, q].reshape(length, BLOCK),
+            preferred_element_type=jnp.float32,
+        )
+
+    for p_at in range(0, total_inputs, BLOCK):
+        p = pl.ds(p_at, BLOCK)
+
+        def column(index, carry, p_at=p_at, p=p):
+            q = pl.ds(pl.multiple_of(index * BLOCK, BLOCK), BLOCK)
+            real = (product(0, 0, p, q) + product(1, 1, p, q)) * scale
+            imag = (product(1, 0, p, q) - product(0, 1, p, q)) * scale
+            result_ref[0, 0, p, q] = real
+            result_ref[0, 1, p, q] = imag
+
+            @pl.when(index * BLOCK > p_at)
+            def _():
+                result_ref[0, 0, q, p] = real.T
+                result_ref[0, 1, q, p] = -imag.T
+
+            return carry
+
+        lax.fori_loop(p_at // BLOCK, total_inputs // BLOCK, column, 0)
+
+
+def correlated(arrived, groups):
+    devices, blocks, planes, steps, inputs = arrived.shape
+    own = planes // 2
+    total_inputs = inputs * groups[1]
+    length = groups[0] * blocks * steps
+    return pl.pallas_call(
+        functools.partial(correlate_kernel, groups, 1.0 / length),
+        grid=(own,),
+        out_shape=jax.ShapeDtypeStruct((own, 2, total_inputs, total_inputs), jnp.float32),
+        in_specs=[pl.BlockSpec(memory_space=pl.ANY)],
+        out_specs=pl.BlockSpec((1, 2, total_inputs, total_inputs), lambda c: (c, 0, 0, 0)),
+        scratch_shapes=[
+            pltpu.VMEM((2, groups[0] * blocks, 2, steps, total_inputs), jnp.bfloat16),
+            pltpu.VMEM((2, total_inputs, length), jnp.bfloat16),
+            pltpu.SemaphoreType.DMA((2,)),
+        ],
+        compiler_params=pltpu.CompilerParams(vmem_limit_bytes=58 * 1024 * 1024),
+        cost_estimate=pl.CostEstimate(
+            flops=own * 8 * length * total_inputs * total_inputs,
+            bytes_accessed=own * 12 * total_inputs * total_inputs,
+            transcendentals=0,
+        ),
+    )(arrived)
+
+
+def fits(volts, taps, groups):
+    taps_count, channels = taps.shape
+    frames = volts.shape[2] // channels
+    return (
+        volts.shape[1] == LANES
+        and channels % BLOCK == 0
+        and frames % STEP == 0
+        and STEP >= taps_count
+        and groups[1] % 2 == 0
+        and volts.size * 2 <= 32 * 1024 * 1024
+    )
+
+
 def per_device(volts, taps):
+    groups = (lax.axis_size("tm"), lax.axis_size("band"))
+    if not fits(volts, taps, groups):
+        return per_device_plain(volts, taps)
+    margin = (taps.shape[0] - 1) * taps.shape[1]
+    history = shifted(volts[:, :, volts.shape[2] - margin :], "tm", 1)
+    arrived = exchanged(volts, history, taps, groups)
+    return correlated(arrived, groups)
+
+
+def per_device_plain(volts, taps):
     time_groups = lax.axis_size("tm")
     band_groups = lax.axis_size("band")
     taps_count = taps.shape[0]

time: 1710 us -> 844 us (0.49)
  blocking collectives: 1110 us -> 0 us
  Pallas kernels: 0 us -> 837 us
  other arithmetic: 278 us -> 2.19 us
  local copies, waits for them, and re-layouts: 197 us -> 3.59 us
  matrix products: 113 us -> 0 us
    all_to_all x2 -> x0, blocking collectives: 1110 us -> none  [the longest x1 734 us: per_device(): lax.all_to_all(lax.all_to_all(spectra, 'tm', split_axis=0, concat_axis=5,...]
    pallas_call x0 -> x2, Pallas kernels: none -> 837 us  [the longest x1 747 us: exchanged(): pl.pallas_call(functools.partial(exchange_kernel, groups), out_shape=jax....]
    convert_element_type x2 -> x0, other arithmetic: 207 us -> none  [the longest x1 173 us: per_device(): filtered = filtered.astype(jnp.bfloat16)]
    dot_general x2 -> x0, matrix products: 113 us -> none  [the longest x1 83 us: square_products(): jnp.einsum('corps,crqs->copq', weighting(signal), signal, preferred_eleme...]
    all_to_all x2 -> x0, local copies, waits for them, and re-layouts: 64.9 us -> none  [the longest x1 42.1 us: per_device(): lax.all_to_all(lax.all_to_all(spectra, 'tm', split_axis=0, concat_axis=5,...]
    convert_element_type x2 -> x0, local copies, waits for them, and re-layouts: 44.8 us -> none  [the longest x1 43.8 us: per_device(): filtered = filtered.astype(jnp.bfloat16)]
    reshape x1 -> x0, local copies, waits for them, and re-layouts: 44.2 us -> none  [per_device(): spectra.astype(jnp.bfloat16)]
    unnamed x5 -> x3, local copies, waits for them, and re-layouts: 41.1 us -> 1.81 us
where the time goes in v1:
time: 844 us
  Pallas kernels  837 us (99%)
    pallas_call x1, Pallas kernels, exchanged(): pl.pallas_call(functools.partial(exchange_kernel, groups), out_shape=jax....  747 us
    pallas_call x1, Pallas kernels, correlated(): pl.pallas_call(functools.partial(correlate_kernel, groups, 1.0 / length),...  90 us
  transfers between devices with their start and end apart: 1, of which 0 were waited for; matrix products, arithmetic and copies ran while one was open for 0% of the time, Pallas kernels for 0%

profile of v1, /device:TPU:3, one launch (start us, length us, event | category | flops | bytes accessed | tf_op | source)
XLA Modules:
  0.0 843.9 jit_solution(4624158155253719771)
XLA Ops:
  0.0 1.2 slice.3
  1.2 1.3 collective-permute-start
  2.5 1.0 fusion.6
  3.5 1.1 negate_convert_fusion
  4.7 0.1 pad_maximum_fusion
  4.8 0.5 copy.4
  5.3 0.9 copy.5
  6.2 0.0 collective-permute-done.history_in_ref
  6.2 0.0 copy-start
  6.2 0.9 copy-done
  7.1 746.7 %shard_map.28.arrived_ref = bf16[32,16,16,16,128]{4,3,2,1,0:T(8,128)(2,1)} custom-call(bf16[2,128,65536]{2,1,0:T(8,128)(2,1)} %volts_ref.1, bf16[2,128,1792]{2,1,0:T(8,128)(2,1)} %copy-done, f32[8,256]{1,0:T(8,128)} %taps_ref.1, bf16[512,512]{1,0:T(8,128)(2,1)} %bitcast.8), custom_call_target="tpu_custom_call" | custom-call | flops 34359738368 | bytes 67108864 | tf_op jit(solution)/shard_map/pallas_call | solution.py:220
  753.9 90.0 %shard_map.29 = f32[8,2,1024,1024]{3,2,1,0:T(8,128)} custom-call(bf16[32,16,16,16,128]{4,3,2,1,0:T(8,128)(2,1)} %shard_map.28.arrived_ref), custom_call_target="tpu_custom_call" | custom-call | flops 68719476736 | bytes 100663296 | tf_op jit(solution)/shard_map/pallas_call | solution.py:323
  (1 shorter events, 0.0 us)
Async XLA Ops:
  1.2 5.0 collective-permute-start
  6.2 0.9 copy-start

commit v2 on v1

--- a/solution.py
+++ b/solution.py
@@ -279,40 +279,31 @@
 
     pltpu.make_async_copy(signal.at[slot], signal.at[slot], sems.at[slot]).wait()
 
-    def turn(index, carry):
-        at = pl.multiple_of(index * LANES, LANES)
-        for part in range(2):
-            piece = signal[slot, :, part, :, pl.ds(at, LANES)].reshape(length, LANES)
-            across[part, pl.ds(at, LANES), :] = piece.T
-        return carry
-
-    lax.fori_loop(0, total_inputs // LANES, turn, 0)
-
-    def product(left, right, p, q):
-        return jnp.dot(
-            across[left, p, :],
-            signal[slot, :, right, :, q].reshape(length, BLOCK),
-            preferred_element_type=jnp.float32,
-        )
-
     for p_at in range(0, total_inputs, BLOCK):
-        p = pl.ds(p_at, BLOCK)
-
-        def column(index, carry, p_at=p_at, p=p):
-            q = pl.ds(pl.multiple_of(index * BLOCK, BLOCK), BLOCK)
-            real = (product(0, 0, p, q) + product(1, 1, p, q)) * scale
-            imag = (product(1, 0, p, q) - product(0, 1, p, q)) * scale
+        panel = p_at // BLOCK % 2
+        p = slice(p_at, p_at + BLOCK)
+        first = signal[slot, :, 0, :, p].reshape(length, BLOCK).T
+        second = signal[slot, :, 1, :, p].reshape(length, BLOCK).T
+        across[panel, 0, :, :length] = first
+        across[panel, 0, :, length:] = second
+        across[panel, 1, :, :length] = second
+        across[panel, 1, :, length:] = -first
+        for q_at in range(p_at, total_inputs, BLOCK):
+            q = slice(q_at, q_at + BLOCK)
+            down = jnp.concatenate(
+                [signal[slot, :, part, :, q].reshape(length, BLOCK) for part in range(2)], axis=0
+            )
+            product = scale * jnp.dot(
+                across[panel].reshape(2 * BLOCK, 2 * length),
+                down,
+                preferred_element_type=jnp.float32,
+            )
+            real, imag = product[:BLOCK], product[BLOCK:]
             result_ref[0, 0, p, q] = real
             result_ref[0, 1, p, q] = imag
-
-            @pl.when(index * BLOCK > p_at)
-            def _():
+            if q_at > p_at:
                 result_ref[0, 0, q, p] = real.T
                 result_ref[0, 1, q, p] = -imag.T
-
-            return carry
-
-        lax.fori_loop(p_at // BLOCK, total_inputs // BLOCK, column, 0)
 
 
 def correlated(arrived, groups):
@@ -328,7 +319,7 @@
         out_specs=pl.BlockSpec((1, 2, total_inputs, total_inputs), lambda c: (c, 0, 0, 0)),
         scratch_shapes=[
             pltpu.VMEM((2, groups[0] * blocks, 2, steps, total_inputs), jnp.bfloat16),
-            pltpu.VMEM((2, total_inputs, length), jnp.bfloat16),
+            pltpu.VMEM((2, 2, BLOCK, 2 * length), jnp.bfloat16),
             pltpu.SemaphoreType.DMA((2,)),
         ],
         compiler_params=pltpu.CompilerParams(vmem_limit_bytes=58 * 1024 * 1024),

time: 844 us -> 810 us (0.960)
  Pallas kernels: 837 us -> 803 us
    pallas_call x1, Pallas kernels: 90 us -> 55.9 us  [correlated(): pl.pallas_call(functools.partial(correlate_kernel, groups, 1.0 / length),...]
where the time goes in v2:
time: 810 us
  Pallas kernels  803 us (99%)
    pallas_call x1, Pallas kernels, exchanged(): pl.pallas_call(functools.partial(exchange_kernel, groups), out_shape=jax....  747 us
    pallas_call x1, Pallas kernels, correlated(): pl.pallas_call(functools.partial(correlate_kernel, groups, 1.0 / length),...  55.9 us
  transfers between devices with their start and end apart: 1, of which 0 were waited for; matrix products, arithmetic and copies ran while one was open for 0% of the time, Pallas kernels for 0%

profile of v2, /device:TPU:3, one launch (start us, length us, event | category | flops | bytes accessed | tf_op | source)
XLA Modules:
  0.0 809.8 jit_solution(4179205976307926195)
XLA Ops:
  0.0 1.2 slice.3
  1.2 1.3 collective-permute-start
  2.5 1.0 fusion.6
  3.5 1.1 negate_convert_fusion
  4.7 0.1 pad_maximum_fusion
  4.8 0.5 copy.4
  5.3 0.9 copy.5
  6.2 0.0 collective-permute-done.history_in_ref
  6.2 0.0 copy-start
  6.2 0.9 copy-done
  7.1 746.7 %shard_map.28.arrived_ref = bf16[32,16,16,16,128]{4,3,2,1,0:T(8,128)(2,1)} custom-call(bf16[2,128,65536]{2,1,0:T(8,128)(2,1)} %volts_ref.1, bf16[2,128,1792]{2,1,0:T(8,128)(2,1)} %copy-done, f32[8,256]{1,0:T(8,128)} %taps_ref.1, bf16[512,512]{1,0:T(8,128)(2,1)} %bitcast.8), custom_call_target="tpu_custom_call" | custom-call | flops 34359738368 | bytes 67108864 | tf_op jit(solution)/shard_map/pallas_call | solution.py:220
  753.9 55.9 %shard_map.29 = f32[8,2,1024,1024]{3,2,1,0:T(8,128)} custom-call(bf16[32,16,16,16,128]{4,3,2,1,0:T(8,128)(2,1)} %shard_map.28.arrived_ref), custom_call_target="tpu_custom_call" | custom-call | flops 68719476736 | bytes 100663296 | tf_op jit(solution)/shard_map/pallas_call | solution.py:314
  (1 shorter events, 0.0 us)
Async XLA Ops:
  1.2 5.0 collective-permute-start
  6.2 0.9 copy-start
